TPU v7x, 32 devices: a whole 2x2x4 slice. The times are simulated.
32 devices in a mesh: gx: 8 (over z, x), gy: 4 (over y, core).
Axes of the slice: x: 2, y: 2, z: 4, core: 2. Of those that a mesh axis runs over, the one named last changes fastest.
Arguments:
- field: bfloat16 [20, 128, 128, 1024], P(None, 'gx', 'gy'), may hold values from -6 to 6
- cotangent: bfloat16 [20, 128, 128, 1024], P(None, 'gx', 'gy'), may hold values from -6 to 6
- spectral_weight: bfloat16 [2, 20, 20, 24, 4608], P(None, None, None, None, ('gy', 'gx')), may hold values from -30 to 30
- local_weight: bfloat16 [20, 20], replicated, may hold values from -1.25 to 1.25
- bias: float32 [20], replicated, may hold values from -4 to 4
Outputs:
- grad_field: bfloat16 [20, 128, 128, 1024], P(None, 'gx', 'gy')
- grad_weight: float32 [2, 20, 20, 24, 4608], P(None, None, None, None, ('gy', 'gx'))
All inputs are finite; a program needn't handle non-finite values.
Results may differ from a plain program's by a relative error of at most 0.03.
Values may be sent and summed in bfloat16 or wider, within the bound.
A program may use at most 256 MiB of HBM per device.

v0:
```python
import math

import jax
import jax.numpy as jnp
from jax import lax
from jax.sharding import PartitionSpec as P

NX = 128
NY = 128
NZ = 128
NT = 8
MS = 24
MT = 8


def axis_tables(length, kept_count, positions):
    half_kept = kept_count // 2
    mode_index = jnp.arange(kept_count, dtype=jnp.int32)
    frequency = jnp.where(mode_index < half_kept, mode_index, mode_index - kept_count)
    phases = jnp.mod(frequency[:, None] * positions[None, :], length)
    angles = phases.astype(jnp.float32) * (2.0 * math.pi / length)
    factor = 1.0 / math.sqrt(length)
    return (
        (jnp.cos(angles) * factor).astype(jnp.bfloat16),
        (jnp.sin(angles) * factor).astype(jnp.bfloat16),
    )


def plane_tables(depth_cells, time_steps, kept_count, kept_time):
    period = depth_cells * time_steps
    positions = jnp.arange(period, dtype=jnp.int32)
    depth_pos = positions // time_steps
    time_pos = positions % time_steps
    mode_index = jnp.arange(kept_count * kept_time, dtype=jnp.int32)
    space_index = mode_index // kept_time
    time_index = mode_index % kept_time
    frequency = jnp.where(space_index < kept_count // 2, space_index, space_index - kept_count)
    phase_depth = jnp.mod(depth_pos[:, None] * frequency[None, :], depth_cells)
    phase_time = jnp.mod(time_pos[:, None] * time_index[None, :], time_steps)
    phases = jnp.mod(phase_depth * time_steps + phase_time * depth_cells, period)
    angles = phases.astype(jnp.float32) * (2.0 * math.pi / period)
    factor = 1.0 / math.sqrt(period)
    return jnp.concatenate([jnp.cos(angles) * factor, -jnp.sin(angles) * factor], axis=1).astype(
        jnp.bfloat16
    )


def forward_axis(values, cos_table, sin_table):
    with_cos = jnp.einsum("kn,lnrm->lrkm", cos_table, values, preferred_element_type=jnp.float32)
    with_sin = jnp.einsum("kn,lnrm->lrkm", sin_table, values, preferred_element_type=jnp.float32)
    real_part = with_cos[:, 0] + with_sin[:, 1]
    imag_part = with_cos[:, 1] - with_sin[:, 0]
    return jnp.stack([real_part, imag_part], axis=1)


def inverse_axis(values, cos_table, sin_table):
    with_cos = jnp.einsum("kn,lrkm->lnrm", cos_table, values, preferred_element_type=jnp.float32)
    with_sin = jnp.einsum("kn,lrkm->lnrm", sin_table, values, preferred_element_type=jnp.float32)
    real_part = with_cos[:, :, 0] - with_sin[:, :, 1]
    imag_part = with_cos[:, :, 1] + with_sin[:, :, 0]
    return jnp.stack([real_part, imag_part], axis=2)


def spectral_apply(weights, mode_values):
    real_weight, imag_weight = (weights[0], weights[1])
    real_mode, imag_mode = (mode_values[:, 0], mode_values[:, 1])
    out_real = jnp.einsum(
        "iokm,ikm->okm", real_weight, real_mode, preferred_element_type=jnp.float32
    ) - jnp.einsum("iokm,ikm->okm", imag_weight, imag_mode, preferred_element_type=jnp.float32)
    out_imag = jnp.einsum(
        "iokm,ikm->okm", real_weight, imag_mode, preferred_element_type=jnp.float32
    ) + jnp.einsum("iokm,ikm->okm", imag_weight, real_mode, preferred_element_type=jnp.float32)
    return jnp.stack([out_real, out_imag], axis=1).astype(jnp.bfloat16)


def spectral_adjoint(weights, mode_values, upstream_modes):
    real_weight, imag_weight = (weights[0], weights[1])
    real_mode = mode_values[:, 0].astype(jnp.float32)
    imag_mode = mode_values[:, 1].astype(jnp.float32)
    real_up = upstream_modes[:, 0].astype(jnp.float32)
    imag_up = upstream_modes[:, 1].astype(jnp.float32)
    grad_real = real_up[None] * real_mode[:, None] + imag_up[None] * imag_mode[:, None]
    grad_imag = imag_up[None] * real_mode[:, None] - real_up[None] * imag_mode[:, None]
    real_low = upstream_modes[:, 0]
    imag_low = upstream_modes[:, 1]
    back_real = jnp.einsum(
        "iokm,okm->ikm", real_weight, real_low, preferred_element_type=jnp.float32
    ) + jnp.einsum("iokm,okm->ikm", imag_weight, imag_low, preferred_element_type=jnp.float32)
    back_imag = jnp.einsum(
        "iokm,okm->ikm", real_weight, imag_low, preferred_element_type=jnp.float32
    ) - jnp.einsum("iokm,okm->ikm", imag_weight, real_low, preferred_element_type=jnp.float32)
    return (jnp.stack([grad_real, grad_imag], axis=0), jnp.stack([back_real, back_imag], axis=1))


def gelu_slope(values):
    return (
        0.5 * (1.0 + lax.erf(values * 0.7071067811865476))
        + values * jnp.exp(-0.5 * values * values) * 0.3989422804014327
    )


def local(field, cotangent, spectral_weight, local_weight, bias):
    channels, width_x, width_y, depth_cells = field.shape
    kept_plane = MS * MT
    plane_table = plane_tables(NZ, NT, MS, MT)
    local_rows = lax.axis_index("gy") * width_y + jnp.arange(width_y, dtype=jnp.int32)
    cos_local, sin_local = axis_tables(NY, MS, local_rows)
    cos_across, sin_across = axis_tables(NX, MS, jnp.arange(NX, dtype=jnp.int32))

    def forward_chain(planes):
        coeffs = jnp.dot(
            planes.reshape(-1, depth_cells), plane_table, preferred_element_type=jnp.float32
        )
        coeffs = coeffs.astype(jnp.bfloat16).reshape(channels * width_x, width_y, 2, kept_plane)
        partial_terms = forward_axis(coeffs, cos_local, sin_local)
        row_modes = lax.psum_scatter(
            partial_terms.astype(jnp.bfloat16), "gy", scatter_dimension=2, tiled=True
        )
        row_modes = row_modes.reshape(channels, width_x, 2, -1)
        blocks = lax.all_to_all(row_modes, "gx", split_axis=3, concat_axis=1, tiled=True)
        return forward_axis(blocks, cos_across, sin_across).astype(jnp.bfloat16)

    def inverse_chain(mode_values):
        across = inverse_axis(mode_values, cos_across, sin_across).astype(jnp.bfloat16)
        row_modes = lax.all_to_all(across, "gx", split_axis=1, concat_axis=3, tiled=True)
        row_modes = row_modes.reshape(channels * width_x, 2, -1, kept_plane)
        all_rows = lax.all_gather(row_modes, "gy", axis=2, tiled=True)
        cell_modes = inverse_axis(all_rows, cos_local, sin_local).astype(jnp.bfloat16)
        flattened = cell_modes.reshape(-1, 2 * kept_plane)
        summed = lax.dot_general(
            flattened, plane_table, (((1,), (1,)), ((), ())), preferred_element_type=jnp.float32
        )
        return summed.reshape(field.shape)

    field_modes = forward_chain(field)
    mixed_modes = spectral_apply(spectral_weight, field_modes)
    spectral = inverse_chain(mixed_modes)
    direct = jnp.einsum("io,ixyp->oxyp", local_weight, field, preferred_element_type=jnp.float32)
    before = spectral + direct + bias[:, None, None, None]
    upstream = (cotangent.astype(jnp.float32) * gelu_slope(before)).astype(jnp.bfloat16)
    upstream_modes = forward_chain(upstream)
    grad_weight, back_modes = spectral_adjoint(spectral_weight, field_modes, upstream_modes)
    returned = inverse_chain(back_modes.astype(jnp.bfloat16))
    direct_back = jnp.einsum(
        "io,oxyp->ixyp", local_weight, upstream, preferred_element_type=jnp.float32
    )
    return ((returned + direct_back).astype(jnp.bfloat16), grad_weight)


def solution(mesh):
    in_specs = (
        P(None, "gx", "gy", None),
        P(None, "gx", "gy", None),
        P(None, None, None, None, ("gy", "gx")),
        P(),
        P(),
    )
    out_specs = (P(None, "gx", "gy", None), P(None, None, None, None, ("gy", "gx")))
    return jax.shard_map(local, mesh=mesh, in_specs=in_specs, out_specs=out_specs, check_vma=False)
```

profile of v0, /device:TPU:0, one launch (start us, length us, event | category | flops | bytes accessed | tf_op | source)
XLA Modules:
  0.0 1111.6 jit_solution(17277798171901574754)
XLA Ops:
  12.9 15.7 %fusion.12 = bf16[10240,384]{0,1:T(8,128)(2,1)} fusion(bf16[10240,1024]{1,0:T(8,128)(2,1)} %bitcast.200, bf16[1024,192]{1,0:T(8,128)(2,1)S(1)} %get-tuple-element.41, bf16[1024,192]{1,0:T(8,128)(2,1)S(1)} %get-tuple-element.40), kind=kOutput, calls=%fused_computation.18 | convolution fusion | flops 8058568704 | bytes 29622272 | tf_op jit(solution)/shard_map/dot_general | solution.py:111
  39.2 22.6 %reshape.131 = bf16[320,32,2,192]{3,2,1,0:T(2,128)(2,1)} reshape(bf16[10240,384]{1,0:T(8,128)(2,1)} %copy.84) | data formatting | bytes 15728640 | tf_op jit(solution)/shard_map/reshape | solution.py:114
  61.8 21.8 %copy.85 = bf16[320,32,2,192]{0,1,3,2:T(8,128)(2,1)} copy(bf16[320,32,2,192]{3,2,1,0:T(2,128)(2,1)} %reshape.131) | data formatting | bytes 15728640 | tf_op jit(solution)/shard_map/reshape | solution.py:114
  112.3 66.5 %reduce-scatter.3.cloned.1.call-done = bf16[320,2,6,192]{0,3,1,2:T(8,128)(2,1)} async-done(((bf16[320,2,24,192]{0,3,1,2:T(8,128)(2,1)}), bf16[320,2,6,192]{0,3,1,2:T(8,128)(2,1)}) %reduce-scatter.3.cloned.1.call-update) | async-done | bytes 1474576 | tf_op jit(solution)/shard_map/reduce_scatter | solution.py:116
  195.2 19.8 %reshape.161 = bf16[8,2,46080]{2,1,0:T(2,128)(2,1)S(1)} reshape(bf16[1152,2,16,20]{3,2,1,0:T(8,128)(2,1)} %bitcast.201) | data formatting | bytes 2949120
  215.0 40.6 %all_to_all.66 = bf16[8,2,46080]{2,1,0:T(2,128)(2,1)S(1)} all-to-all(bf16[8,2,46080]{2,1,0:T(2,128)(2,1)S(1)} %reshape.161), channel_id=1, replica_groups=mesh['gx'=8,'gy'=4] {'gx'}, dimensions={0} | all-to-all | bytes 2949120 | tf_op jit(solution)/shard_map/all_to_all | solution.py:120
  255.6 24.4 %reshape.162 = bf16[1152,2,16,20]{3,2,1,0:T(8,128)(2,1)} reshape(bf16[8,2,46080]{2,1,0:T(2,128)(2,1)S(1)} %all_to_all.66) | data formatting | bytes 2949120
  280.0 13.2 %copy.91 = bf16[20,8,16,2,144]{4,2,1,3,0:T(8,128)(2,1)S(1)} copy(bf16[20,8,16,2,144]{0,2,3,4,1:T(8,128)(2,1)} %bitcast.202) | data formatting | bytes 2949120 | tf_op jit(solution)/shard_map/all_to_all | solution.py:120
  311.4 62.5 %all_to_all.67 = bf16[20,128,2,144]{3,2,0,1:T(2,128)(2,1)S(1)} all-to-all(bf16[20,128,2,144]{3,2,0,1:T(2,128)(2,1)S(1)} %copy.94), channel_id=1, replica_groups=mesh['gx'=8,'gy'=4] {'gx'}, dimensions={1} | all-to-all | bytes 2949120 | tf_op jit(solution)/shard_map/all_to_all | solution.py:125
  386.4 30.6 %fusion.10 = f32[20,16,32,1024]{3,0,2,1:T(8,128)} fusion(bf16[20,16,32,1024]{3,2,1,0:T(8,128)(2,1)} %param.5, bf16[20,20]{1,0:T(8,128)(2,1)S(1)} %copy-done), kind=kOutput, calls=%fused_computation.13 | convolution fusion | flops 419430400 | bytes 62915360 | tf_op jit(solution)/shard_map/io,ixyp->oxyp/dot_general | solution.py:138
  416.9 18.3 %all-gather.3.cloned.1.call-done = bf16[320,2,24,192]{0,3,1,2:T(8,128)(2,1)} async-done(((bf16[320,2,6,192]{0,3,1,2:T(8,128)(2,1)}), bf16[320,2,24,192]{0,3,1,2:T(8,128)(2,1)}) %all-gather.3.cloned.1.call-update) | async-done | bytes 5898256 | tf_op jit(solution)/shard_map/all_gather | solution.py:127
  443.7 14.4 %convolution_bitcast_fusion.3 = f32[320,32,2,192]{0,1,3,2:T(8,128)} fusion(bf16[320,2,24,192]{0,3,1,2:T(8,128)(2,1)} %all-gather.3.cloned.1.call-done, s32[32]{0:T(128)S(1)} %iota_add_fusion, s32[24]{0:T(128)S(1)} %compare_select_fusion.1), kind=kOutput, calls=%fused_computation.60 | convolution fusion | flops 188755968 | bytes 21627104 | tf_op jit(solution)/shard_map/kn,lrkm->lnrm/dot_general | solution.py:57
  458.2 11.5 %fusion.24 = (bf16[320,32,1,192]{0,1,3,2:T(8,128)(2,1)}, bf16[320,32,1,192]{0,1,3,2:T(8,128)(2,1)}) fusion(f32[320,32,2,192]{0,1,3,2:T(8,128)S(1)} %convolution_bitcast_fusion.2, f32[320,32,2,192]{0,1,3,2:T(8,128)} %convolution_bitcast_fusion.3), kind=kLoop, calls=%fused_computation.44 | loop fusion | flops 7864320 | bytes 39321600 | tf_op jit(solution)/shard_map/convert.16
  479.0 22.8 %copy.100 = bf16[320,32,2,192]{3,2,1,0:T(2,128)(2,1)} copy(bf16[320,32,2,192]{0,1,3,2:T(8,128)(2,1)} %pad_maximum_fusion.1) | data formatting | bytes 15728640 | tf_op jit(solution)/shard_map/stack | solution.py:61
  501.8 21.1 %convert_element_type.116 = bf16[20,16,32,384]{3,2,1,0:T(8,128)(2,1)} reshape(bf16[320,32,2,192]{3,2,1,0:T(2,128)(2,1)} %copy.100) | data formatting | bytes 15728640 | tf_op jit(solution)/shard_map/convert_element_type | solution.py:128
  523.0 49.9 %fusion.5 = bf16[20,16,32,1024]{3,2,1,0:T(8,128)(2,1)} fusion(f32[20,16,32,1024]{3,0,2,1:T(8,128)} %fusion.10, bf16[20,16,32,1024]{3,2,1,0:T(8,128)(2,1)} %param.6, f32[20]{0:T(128)S(1)} %copy-done.11, bf16[20,16,32,384]{3,2,1,0:T(8,128)(2,1)} %convert_element_type.116, bf16[1024,192]{1,0:T(8,128)(2,1)S(1)} %copy-done.7, bf16[1024,192]{1,0:T(8,128)(2,1)S(1)} %copy-done.4), kind=kOutput, calls=%fused_computation.6 | convolution fusion | flops 8190951424 | bytes 92536912 | tf_op jit(solution)/shard_map/dot_general | solution.py:130
  572.9 17.3 %convolution_convert_fusion.1 = bf16[10240,384]{1,0:T(8,128)(2,1)} fusion(bf16[10240,1024]{1,0:T(8,128)(2,1)} %bitcast.205, bf16[1024,192]{1,0:T(8,128)(2,1)S(1)} %copy-done.7, bf16[1024,192]{1,0:T(8,128)(2,1)S(1)} %copy-done.4), kind=kOutput, calls=%fused_computation.17 | convolution fusion | flops 8058568704 | bytes 29622272 | tf_op jit(solution)/shard_map/dot_general | solution.py:111
  590.2 22.8 %reshape.135 = bf16[320,32,2,192]{3,2,1,0:T(2,128)(2,1)} reshape(bf16[10240,384]{1,0:T(8,128)(2,1)} %convolution_convert_fusion.1) | data formatting | bytes 15728640 | tf_op jit(solution)/shard_map/reshape | solution.py:114
  613.0 21.9 %copy.104 = bf16[320,32,2,192]{0,1,3,2:T(8,128)(2,1)} copy(bf16[320,32,2,192]{3,2,1,0:T(2,128)(2,1)} %reshape.135) | data formatting | bytes 15728640 | tf_op jit(solution)/shard_map/reshape | solution.py:114
  663.2 63.7 %reduce-scatter.5.cloned.1.call-done = bf16[320,2,6,192]{0,3,1,2:T(8,128)(2,1)} async-done(((bf16[320,2,24,192]{0,3,1,2:T(8,128)(2,1)}), bf16[320,2,6,192]{0,3,1,2:T(8,128)(2,1)}) %reduce-scatter.5.cloned.1.call-update) | async-done | bytes 1474576 | tf_op jit(solution)/shard_map/reduce_scatter | solution.py:116
  743.4 19.8 %reshape.163 = bf16[8,2,46080]{2,1,0:T(2,128)(2,1)S(1)} reshape(bf16[1152,2,16,20]{3,2,1,0:T(8,128)(2,1)} %bitcast.203) | data formatting | bytes 2949120
  763.1 40.8 %all_to_all.68 = bf16[8,2,46080]{2,1,0:T(2,128)(2,1)S(1)} all-to-all(bf16[8,2,46080]{2,1,0:T(2,128)(2,1)S(1)} %reshape.163), channel_id=1, replica_groups=mesh['gx'=8,'gy'=4] {'gx'}, dimensions={0} | all-to-all | bytes 2949120 | tf_op jit(solution)/shard_map/all_to_all | solution.py:120
  804.0 24.4 %reshape.164 = bf16[1152,2,16,20]{3,2,1,0:T(8,128)(2,1)} reshape(bf16[8,2,46080]{2,1,0:T(2,128)(2,1)S(1)} %all_to_all.68) | data formatting | bytes 2949120
  828.4 13.2 %copy.110 = bf16[20,8,16,2,144]{4,2,1,3,0:T(8,128)(2,1)S(1)} copy(bf16[20,8,16,2,144]{0,2,3,4,1:T(8,128)(2,1)} %bitcast.204) | data formatting | bytes 2949120 | tf_op jit(solution)/shard_map/all_to_all | solution.py:120
  860.3 62.7 %all_to_all.69 = bf16[20,128,2,144]{3,2,0,1:T(2,128)(2,1)S(1)} all-to-all(bf16[20,128,2,144]{3,2,0,1:T(2,128)(2,1)S(1)} %copy.113), channel_id=1, replica_groups=mesh['gx'=8,'gy'=4] {'gx'}, dimensions={1} | all-to-all | bytes 2949120 | tf_op jit(solution)/shard_map/all_to_all | solution.py:125
  935.4 28.4 %fusion.8 = f32[16,32,1024,20]{2,3,1,0:T(8,128)} fusion(bf16[20,16,32,1024]{3,2,1,0:T(8,128)(2,1)} %fusion.5, bf16[20,20]{1,0:T(8,128)(2,1)S(1)} %copy-done), kind=kOutput, calls=%fused_computation.11 | convolution fusion | flops 419430400 | bytes 62915360 | tf_op jit(solution)/shard_map/io,oxyp->ixyp/dot_general | solution.py:144
  970.8 11.4 %pad_maximum_fusion = f32[2,20,20,24,144]{4,3,2,1,0:T(8,128)} fusion(f32[1,20,20,24,144]{4,3,2,1,0:T(8,128)} %get-tuple-element.35, f32[1,20,20,24,144]{4,3,2,1,0:T(8,128)S(1)} %get-tuple-element.34), kind=kLoop, calls=%fused_computation.15 | loop fusion | flops 2764800 | bytes 22118400 | tf_op jit(solution)/shard_map/stack | solution.py:92
  992.6 14.4 %convolution_bitcast_fusion.1 = f32[320,32,2,192]{0,1,3,2:T(8,128)} fusion(bf16[320,2,24,192]{0,3,1,2:T(8,128)(2,1)} %all-gather.5.cloned.1.call-done, s32[32]{0:T(128)S(1)} %iota_add_fusion, s32[24]{0:T(128)S(1)} %compare_select_fusion.1), kind=kOutput, calls=%fused_computation.58 | convolution fusion | flops 188755968 | bytes 21627104 | tf_op jit(solution)/shard_map/kn,lrkm->lnrm/dot_general | solution.py:57
  1007.1 11.5 %fusion.22 = (bf16[320,32,1,192]{0,1,3,2:T(8,128)(2,1)}, bf16[320,32,1,192]{0,1,3,2:T(8,128)(2,1)}) fusion(f32[320,32,2,192]{0,1,3,2:T(8,128)S(1)} %convolution_bitcast_fusion, f32[320,32,2,192]{0,1,3,2:T(8,128)} %convolution_bitcast_fusion.1), kind=kLoop, calls=%fused_computation.40 | loop fusion | flops 7864320 | bytes 39321600 | tf_op jit(solution)/shard_map/convert.2
  1027.8 22.8 %copy.119 = bf16[320,32,2,192]{3,2,1,0:T(2,128)(2,1)} copy(bf16[320,32,2,192]{0,1,3,2:T(8,128)(2,1)} %pad_maximum_fusion.2) | data formatting | bytes 15728640 | tf_op jit(solution)/shard_map/stack | solution.py:61
  1050.6 21.3 %convert_element_type.119 = bf16[20,16,32,384]{3,2,1,0:T(8,128)(2,1)} reshape(bf16[320,32,2,192]{3,2,1,0:T(2,128)(2,1)} %copy.119) | data formatting | bytes 15728640 | tf_op jit(solution)/shard_map/convert_element_type | solution.py:128
  1071.9 32.8 %fusion.6 = bf16[20,16,32,1024]{3,2,1,0:T(8,128)(2,1)} fusion(f32[16,32,1024,20]{2,3,1,0:T(8,128)} %fusion.8, bf16[20,16,32,384]{3,2,1,0:T(8,128)(2,1)} %convert_element_type.119, bf16[1024,192]{1,0:T(8,128)(2,1)S(1)} %copy-done.8, bf16[1024,192]{1,0:T(8,128)(2,1)S(1)} %copy-done.5), kind=kOutput, calls=%fused_computation.8 | convolution fusion | flops 8075608064 | bytes 71565312 | tf_op jit(solution)/shard_map/dot_general | solution.py:130
  (94 shorter events, 212.0 us)
Async XLA Ops:
  7.2 379.2 %copy-start = (bf16[20,20]{1,0:T(8,128)(2,1)S(1)}, bf16[20,20]{1,0:T(8,128)(2,1)}, u32[]{:S(2)}) copy-start(bf16[20,20]{1,0:T(8,128)(2,1)} %param.8) | copy-start | bytes 2404
  7.2 171.6 %reduce-scatter.3.cloned.1.call-start = ((), (), s32[]{:S(2)}) async-start(), calls=%async_computation.6 | async-start | bytes 8847360 | tf_op jit(solution)/shard_map/reduce_scatter | solution.py:116
  12.9 15.7 %copy-start.3 = (bf16[1024,192]{1,0:T(8,128)(2,1)}, bf16[1024,192]{1,0:T(8,128)(2,1)S(1)}, u32[]{:S(2)}) copy-start(bf16[1024,192]{1,0:T(8,128)(2,1)S(1)} %get-tuple-element.40) | copy-start | bytes 1179652
  12.9 15.7 %copy-start.6 = (bf16[1024,192]{1,0:T(8,128)(2,1)}, bf16[1024,192]{1,0:T(8,128)(2,1)S(1)}, u32[]{:S(2)}) copy-start(bf16[1024,192]{1,0:T(8,128)(2,1)S(1)} %get-tuple-element.41) | copy-start | bytes 1179652
  83.6 6.4 copy-start.1
  112.2 323.0 %all-gather.3.cloned.1.call-start = ((), (), s32[]{:S(2)}) async-start(), calls=%async_computation.7 | async-start | bytes 8847360 | tf_op jit(solution)/shard_map/all_gather | solution.py:127
  386.3 340.6 %reduce-scatter.5.cloned.1.call-start = ((), (), s32[]{:S(2)}) async-start(), calls=%async_computation.8 | async-start | bytes 8847360 | tf_op jit(solution)/shard_map/reduce_scatter | solution.py:116
  501.8 21.1 %copy-start.4 = (bf16[1024,192]{1,0:T(8,128)(2,1)S(1)}, bf16[1024,192]{1,0:T(8,128)(2,1)}, u32[]{:S(2)}) copy-start(bf16[1024,192]{1,0:T(8,128)(2,1)} %copy-done.3) | copy-start | bytes 1179652
  501.8 21.1 %copy-start.7 = (bf16[1024,192]{1,0:T(8,128)(2,1)S(1)}, bf16[1024,192]{1,0:T(8,128)(2,1)}, u32[]{:S(2)}) copy-start(bf16[1024,192]{1,0:T(8,128)(2,1)} %copy-done.6) | copy-start | bytes 1179652
  501.8 21.1 %copy-start.11 = (f32[20]{0:T(128)S(1)}, f32[20]{0:T(128)}, u32[]{:S(2)}) copy-start(f32[20]{0:T(128)} %param.9) | copy-start | bytes 244
  635.0 6.4 copy-start.2
  663.1 321.2 %all-gather.5.cloned.1.call-start = ((), (), s32[]{:S(2)}) async-start(), calls=%async_computation.9 | async-start | bytes 8847360 | tf_op jit(solution)/shard_map/all_gather | solution.py:127
  935.4 28.4 %copy-start.9 = (f32[20,24,144]{2,1,0:T(8,128)S(1)}, f32[20,24,144]{2,1,0:T(8,128)}, u32[]{:S(2)}) copy-start(f32[20,24,144]{2,1,0:T(8,128)} %get-tuple-element.16) | copy-start | bytes 829444
  935.4 28.4 %copy-start.10 = (f32[20,24,144]{2,1,0:T(8,128)S(1)}, f32[20,24,144]{2,1,0:T(8,128)}, u32[]{:S(2)}) copy-start(f32[20,24,144]{2,1,0:T(8,128)} %get-tuple-element.38) | copy-start | bytes 829444
  1050.5 21.4 %copy-start.5 = (bf16[1024,192]{1,0:T(8,128)(2,1)S(1)}, bf16[1024,192]{1,0:T(8,128)(2,1)}, u32[]{:S(2)}) copy-start(bf16[1024,192]{1,0:T(8,128)(2,1)} %copy-done.3) | copy-start | bytes 1179652
  1050.6 21.4 %copy-start.8 = (bf16[1024,192]{1,0:T(8,128)(2,1)S(1)}, bf16[1024,192]{1,0:T(8,128)(2,1)}, u32[]{:S(2)}) copy-start(bf16[1024,192]{1,0:T(8,128)(2,1)} %copy-done.6) | copy-start | bytes 1179652
Sparse Core Ops, SparseCore 0:
  112.3 66.3 reduce-scatter.2
  386.4 48.8 all-gather.2
  663.2 63.6 reduce-scatter.4
  935.5 48.7 all-gather.4
where the time goes:
time: 1130 us; the launch traced here: 1110 us
  local copies, waits for them, and re-layouts  382 us (34%)
  matrix products  250 us (22%)
  blocking collectives  207 us (18%)
  waiting for transfers between devices  151 us (13%)
  other arithmetic  108 us (10%)
  between operations  14.6 us (1%)
    reduce_scatter x2, waiting for transfers between devices, forward_chain(): lax.psum_scatter(partial_terms.astype(jnp.bfloat16), 'gy', scatter_dimens...  130 us
    all_to_all x2, blocking collectives, inverse_chain(): lax.all_to_all(across, 'gx', split_axis=1, concat_axis=3, tiled=True)  125 us
    unnamed x28, local copies, waits for them, and re-layouts  89.6 us
    reshape x4, local copies, waits for them, and re-layouts, forward_chain(): coeffs.astype(jnp.bfloat16)  89.2 us
    dot_general x2, matrix products, inverse_chain(): lax.dot_general(flattened, plane_table, (((1,), (1,)), ((), ())), preferr...  82.7 us
    all_to_all x2, blocking collectives, forward_chain(): lax.all_to_all(row_modes, 'gx', split_axis=3, concat_axis=1, tiled=True)  81.5 us
    another operation x4, local copies, waits for them, and re-layouts, inverse_axis(): return jnp.stack([real_part, imag_part], axis=2)  57.4 us
    another operation x7, other arithmetic  44.7 us
  transfers between devices with their start and end apart: 4, of which 4 were waited for; matrix products, arithmetic and copies ran while one was open for 7% of the time, Pallas kernels for 0%

commit v1 on v0

--- a/solution.py
+++ b/solution.py
@@ -1,8 +1,11 @@
+import functools
 import math
 
 import jax
 import jax.numpy as jnp
 from jax import lax
+from jax.experimental import pallas as pl
+from jax.experimental.pallas import tpu as pltpu
 from jax.sharding import PartitionSpec as P
 
 NX = 128
@@ -147,6 +150,391 @@
     return ((returned + direct_back).astype(jnp.bfloat16), grad_weight)
 
 
+def kernel_tables(width_x, gx_size):
+    group = lax.axis_index("gy")
+    share = MS // 4
+    order = jnp.array([0, 2, 1, 3], dtype=jnp.int32)
+    owners = jnp.bitwise_xor(group, order)
+    kept_rows = (owners[:, None] * share + jnp.arange(share, dtype=jnp.int32)[None, :]).reshape(-1)
+    cells = NY // 4
+    local_rows = group * cells + jnp.arange(cells, dtype=jnp.int32)
+    cos_rows, sin_rows = axis_tables(NY, MS, local_rows)
+    eye_x = jnp.eye(8, dtype=jnp.bfloat16)
+
+    def spread(table):
+        table = jnp.take(table, kept_rows, axis=0)
+        return (table[:, None, None, :] * eye_x[None, :, :, None]).reshape(MS * 8, 8 * cells)
+
+    row_table = jnp.concatenate([spread(cos_rows), spread(sin_rows)], axis=0)
+    cos_x, sin_x = axis_tables(NX, MS, jnp.arange(NX, dtype=jnp.int32))
+    parts = jnp.stack(
+        [jnp.stack([cos_x, sin_x], axis=0), jnp.stack([-sin_x, cos_x], axis=0)], axis=0
+    ).reshape(2, 2, MS, gx_size, width_x)
+    eye_c = jnp.eye(4, dtype=jnp.bfloat16)
+    across = parts.transpose(0, 2, 3, 1, 4)[:, None, :, :, :, None, :] * eye_c[
+        None, :, None, None, None, :, None
+    ]
+    return row_table, across.reshape(2 * 4 * MS, gx_size * 2 * 4 * width_x)
+
+
+def params(semantics=("arbitrary",)):
+    return pltpu.CompilerParams(dimension_semantics=semantics, vmem_limit_bytes=56 * 1024 * 1024)
+
+
+def whole(shape):
+    return pl.BlockSpec(shape, lambda *_: (0,) * len(shape))
+
+
+def rows_kernel(planes_ref, plane_ref, row_ref, near_ref, far_ref):
+    count, width_x, cells, depth = planes_ref.shape
+    kept = MS * MT
+    rows = 8 * cells
+    half = MS // 2
+    for c in range(count):
+        pieces = []
+        for g in range(width_x // 8):
+            seg = planes_ref[c, g * 8 : g * 8 + 8].reshape(rows, depth)
+            modes = jnp.dot(seg, plane_ref[...], preferred_element_type=jnp.float32)
+            both = jnp.dot(
+                row_ref[...], modes.astype(jnp.bfloat16), preferred_element_type=jnp.float32
+            )
+            top, low = both[: MS * 8], both[MS * 8 :]
+            real = top[:, :kept] + low[:, 256 : 256 + kept]
+            imag = top[:, 256 : 256 + kept] - low[:, :kept]
+            pieces.append(jnp.concatenate([real, imag], axis=1).reshape(MS, 8, 2 * kept))
+        out = jnp.concatenate(pieces, axis=1).astype(jnp.bfloat16)
+        near_ref[:, c] = out[:half]
+        far_ref[:, c] = out[half:]
+
+
+def rows_call(planes, first, count, plane_pad, row_table):
+    _, width_x, cells, depth = planes.shape
+    step = 2
+    kept = MS * MT
+    half = MS // 2
+    out = jax.ShapeDtypeStruct((half, count, width_x, 2 * kept), jnp.bfloat16)
+    block = pl.BlockSpec((half, step, width_x, 2 * kept), lambda s: (0, s, 0, 0))
+    flops = 2 * count * width_x * cells * depth * 2 * kept
+    return pl.pallas_call(
+        rows_kernel,
+        grid=(count // step,),
+        in_specs=[
+            pl.BlockSpec((step, width_x, cells, depth), lambda s: (first // step + s, 0, 0, 0)),
+            whole(plane_pad.shape),
+            whole(row_table.shape),
+        ],
+        out_specs=[block, block],
+        out_shape=[out, out],
+        compiler_params=params(),
+        cost_estimate=pl.CostEstimate(
+            flops=2 * flops, bytes_accessed=2 * count * width_x * cells * depth, transcendentals=0
+        ),
+    )(planes, plane_pad, row_table)
+
+
+def pack_kernel(own_ref, other_ref, out_ref):
+    _, count, width_x, lanes = own_ref.shape
+    kept = lanes // 2
+    for u in range(count // 4):
+        value = own_ref[0, 4 * u : 4 * u + 4].astype(jnp.float32)
+        value = value + other_ref[0, 4 * u : 4 * u + 4].astype(jnp.float32)
+        value = value.reshape(4 * width_x, lanes)
+        stacked = jnp.concatenate([value[:, :kept], value[:, kept:]], axis=0)
+        out_ref[:, u * 128 : u * 128 + 128] = stacked.T.astype(jnp.bfloat16)
+
+
+def pack_call(own, other):
+    share, count, width_x, lanes = other.shape
+    block = pl.BlockSpec((1, count, width_x, lanes), lambda s: (s, 0, 0, 0))
+    kept = lanes // 2
+    return pl.pallas_call(
+        pack_kernel,
+        grid=(share,),
+        in_specs=[block, block],
+        out_specs=pl.BlockSpec((kept, count * 32), lambda s: (s, 0)),
+        out_shape=jax.ShapeDtypeStruct((share * kept, count * 32), jnp.bfloat16),
+        compiler_params=params(),
+        cost_estimate=pl.CostEstimate(
+            flops=other.size, bytes_accessed=other.size * 6, transcendentals=0
+        ),
+    )(own, other)
+
+
+def unpack_kernel(in_ref, out_ref):
+    _, count, width_x, lanes = out_ref.shape
+    for u in range(count // 4):
+        value = in_ref[:, u * 128 : u * 128 + 128].astype(jnp.float32).T
+        value = jnp.concatenate([value[: 4 * width_x], value[4 * width_x :]], axis=1)
+        out_ref[0, 4 * u : 4 * u + 4] = value.reshape(4, width_x, lanes).astype(jnp.bfloat16)
+
+
+def unpack_call(packed, width_x):
+    kept = MS * MT
+    share = packed.shape[0] // kept
+    count = packed.shape[1] // 32
+    return pl.pallas_call(
+        unpack_kernel,
+        grid=(share,),
+        in_specs=[pl.BlockSpec((kept, count * 32), lambda s: (s, 0))],
+        out_specs=pl.BlockSpec((1, count, width_x, 2 * kept), lambda s: (s, 0, 0, 0)),
+        out_shape=jax.ShapeDtypeStruct((share, count, width_x, 2 * kept), jnp.bfloat16),
+        compiler_params=params(),
+        cost_estimate=pl.CostEstimate(
+            flops=packed.size, bytes_accessed=packed.size * 4, transcendentals=0
+        ),
+    )(packed)
+
+
+def gather_modes(in_refs, table_ref, modes_ref):
+    span = modes_ref.shape[-1]
+    c = 0
+    for ref in in_refs:
+        sources = ref.shape[0] // span
+        for u in range(ref.shape[1] // 128):
+            values = jnp.concatenate(
+                [ref[g * span : g * span + span, u * 128 : u * 128 + 128] for g in range(sources)],
+                axis=1,
+            )
+            found = lax.dot_general(
+                table_ref[...], values, (((1,), (1,)), ((), ())), preferred_element_type=jnp.float32
+            )
+            found = found.astype(jnp.bfloat16).astype(jnp.float32)
+            modes_ref[:, c : c + 4] = found.reshape(2, 4, MS, span)
+            c += 4
+
+
+def scatter_modes(modes_ref, table_ref, out_refs):
+    span = modes_ref.shape[-1]
+    c = 0
+    for ref in out_refs:
+        sources = ref.shape[0] // span
+        for u in range(ref.shape[1] // 128):
+            values = modes_ref[:, c : c + 4].reshape(2 * 4 * MS, span).astype(jnp.bfloat16)
+            cells = lax.dot_general(
+                values, table_ref[...], (((0,), (0,)), ((), ())), preferred_element_type=jnp.float32
+            ).astype(jnp.bfloat16)
+            for g in range(sources):
+                ref[g * span : g * span + span, u * 128 : u * 128 + 128] = cells[
+                    :, g * 128 : g * 128 + 128
+                ]
+            c += 4
+
+
+def apply_kernel(pieces, *refs):
+    in_refs, (table_ref, weight_ref, modes_ref) = refs[:pieces], refs[pieces : pieces + 3]
+    out_refs, mixed_ref = refs[pieces + 3 : -1], refs[-1]
+    channels = modes_ref.shape[1]
+    step = pl.program_id(0)
+
+    @pl.when(step == 0)
+    def _():
+        gather_modes(in_refs, table_ref, modes_ref)
+
+    real = jnp.zeros(modes_ref.shape[2:], jnp.float32)
+    imag = real
+    for i in range(channels):
+        real_weight = weight_ref[0, i, 0].astype(jnp.float32)
+        imag_weight = weight_ref[1, i, 0].astype(jnp.float32)
+        real_mode, imag_mode = modes_ref[0, i], modes_ref[1, i]
+        real = real + real_weight * real_mode - imag_weight * imag_mode
+        imag = imag + real_weight * imag_mode + imag_weight * real_mode
+    mixed_ref[0, step] = real
+    mixed_ref[1, step] = imag
+
+    @pl.when(step == channels - 1)
+    def _():
+        scatter_modes(mixed_ref, table_ref, out_refs)
+
+
+def apply_call(blocks, table, weight):
+    _, channels, _, _, span = weight.shape
+    modes = (2, channels, MS, span)
+    return pl.pallas_call(
+        functools.partial(apply_kernel, len(blocks)),
+        grid=(channels,),
+        in_specs=[whole(b.shape) for b in blocks]
+        + [
+            whole(table.shape),
+            pl.BlockSpec((2, channels, 1, MS, span), lambda s: (0, 0, s, 0, 0)),
+        ],
+        out_specs=[whole(modes)] + [whole(b.shape) for b in blocks],
+        out_shape=[jax.ShapeDtypeStruct(modes, jnp.float32)]
+        + [jax.ShapeDtypeStruct(b.shape, jnp.bfloat16) for b in blocks],
+        scratch_shapes=[pltpu.VMEM(modes, jnp.float32)],
+        compiler_params=params(),
+    )(*blocks, table, weight)
+
+
+def adjoint_kernel(pieces, *refs):
+    in_refs = refs[:pieces]
+    table_ref, weight_ref, modes_ref, grad_ref = refs[pieces : pieces + 4]
+    out_refs, up_ref, back_ref = refs[pieces + 4 : -2], refs[-2], refs[-1]
+    channels = modes_ref.shape[1]
+    step = pl.program_id(0)
+
+    @pl.when(step == 0)
+    def _():
+        gather_modes(in_refs, table_ref, up_ref)
+
+    real_mode, imag_mode = modes_ref[0, step], modes_ref[1, step]
+    real = jnp.zeros(modes_ref.shape[2:], jnp.float32)
+    imag = real
+    for o in range(channels):
+        real_up, imag_up = up_ref[0, o], up_ref[1, o]
+        grad_ref[0, 0, o] = real_up * real_mode + imag_up * imag_mode
+        grad_ref[1, 0, o] = imag_up * real_mode - real_up * imag_mode
+        real_weight = weight_ref[0, 0, o].astype(jnp.float32)
+        imag_weight = weight_ref[1, 0, o].astype(jnp.float32)
+        real = real + real_weight * real_up + imag_weight * imag_up
+        imag = imag + real_weight * imag_up - imag_weight * real_up
+    back_ref[0, step] = real
+    back_ref[1, step] = imag
+
+    @pl.when(step == channels - 1)
+    def _():
+        scatter_modes(back_ref, table_ref, out_refs)
+
+
+def adjoint_call(blocks, table, weight, modes):
+    _, channels, _, _, span = weight.shape
+    spec = pl.BlockSpec((2, 1, channels, MS, span), lambda s: (0, s, 0, 0, 0))
+    return pl.pallas_call(
+        functools.partial(adjoint_kernel, len(blocks)),
+        grid=(channels,),
+        in_specs=[whole(b.shape) for b in blocks] + [whole(table.shape), spec, whole(modes.shape)],
+        out_specs=[spec] + [whole(b.shape) for b in blocks],
+        out_shape=[jax.ShapeDtypeStruct(weight.shape, jnp.float32)]
+        + [jax.ShapeDtypeStruct(b.shape, jnp.bfloat16) for b in blocks],
+        scratch_shapes=[pltpu.VMEM(modes.shape, jnp.float32)] * 2,
+        compiler_params=params(),
+    )(*blocks, table, weight, modes)
+
+
+def cells_kernel(counts, with_slope, *refs):
+    pieces = 4 * len(counts)
+    mode_refs, (row_ref, plane_ref, mix_ref, planes_ref) = refs[:pieces], refs[pieces : pieces + 4]
+    rest, out_ref, cell_ref = refs[pieces + 4 : -2], refs[-2], refs[-1]
+    channels, _, tall, depth = planes_ref.shape
+    kept = MS * MT
+    step = pl.program_id(0)
+    cells = row_ref.shape[0] // 8
+
+    @pl.when(step == 0)
+    def _():
+        first = 0
+        for at, count in enumerate(counts):
+            refs_of = mode_refs[4 * at : 4 * at + 4]
+
+            def body(c, carry, first=first, refs_of=refs_of):
+                value = jnp.concatenate([ref[:, c] for ref in refs_of], axis=0).astype(jnp.float32)
+                for g in range(value.shape[1] // 8):
+                    part = value[:, g * 8 : g * 8 + 8].reshape(MS * 8, 2 * kept)
+                    turned = jnp.concatenate([-part[:, kept:], part[:, :kept]], axis=1)
+                    both = jnp.concatenate([part, turned], axis=0).astype(jnp.bfloat16)
+                    cell_ref[g, first + c] = jnp.dot(
+                        row_ref[...], both, preferred_element_type=jnp.float32
+                    ).astype(jnp.bfloat16)
+                return carry
+
+            lax.fori_loop(0, count, body, 0)
+            first += count
+
+    parts = cells // tall
+    x = step // parts
+    row = pl.multiple_of((x % 8) * cells + (step % parts) * tall, tall)
+    modes = cell_ref[x // 8, :, pl.ds(row, tall), :].reshape(channels * tall, 2 * kept)
+    planes = planes_ref[...].reshape(channels * tall, depth)
+    value = jnp.dot(modes, plane_ref[...], preferred_element_type=jnp.float32)
+    value = value + jnp.dot(mix_ref[...], planes, preferred_element_type=jnp.float32)
+    if with_slope:
+        cot_ref, bias_ref = rest
+        value = value + bias_ref[...]
+        cot = cot_ref[...].reshape(channels * tall, depth).astype(jnp.float32)
+        value = cot * gelu_slope(value)
+    out_ref[...] = value.astype(jnp.bfloat16).reshape(out_ref.shape)
+
+
+def cells_call(pieces, row_table, plane_back, mix, planes, cotangent=None, bias=None):
+    channels, width_x, cells, depth = planes.shape
+    kept = MS * MT
+    tall = 16
+    parts = cells // tall
+    counts = tuple(group[0].shape[1] for group in pieces)
+    flat = [p for group in pieces for p in group]
+    spec = pl.BlockSpec((channels, 1, tall, depth), lambda s: (0, s // parts, s % parts, 0))
+    extra = [] if bias is None else [cotangent, jnp.repeat(bias, tall)[:, None]]
+    extra_specs = [] if bias is None else [spec, whole((channels * tall, 1))]
+    mixing = (mix[:, None, :, None] * jnp.eye(tall, dtype=mix.dtype)[None, :, None, :]).reshape(
+        channels * tall, channels * tall
+    )
+    return pl.pallas_call(
+        functools.partial(cells_kernel, counts, bias is not None),
+        grid=(width_x * parts,),
+        in_specs=[whole(p.shape) for p in flat]
+        + [whole(row_table.shape), whole(plane_back.shape), whole(mixing.shape), spec]
+        + extra_specs,
+        out_specs=spec,
+        out_shape=jax.ShapeDtypeStruct(planes.shape, jnp.bfloat16),
+        scratch_shapes=[
+            pltpu.VMEM((width_x // 8, channels, 8 * cells, 2 * kept), jnp.bfloat16)
+        ],
+        compiler_params=params(),
+    )(*flat, row_table, plane_back, mixing, planes, *extra)
+
+
+def local_kernels(field, cotangent, spectral_weight, local_weight, bias):
+    channels, width_x, cells, depth = field.shape
+    gx_size = NX // width_x
+    kept = MS * MT
+    plane_table = plane_tables(NZ, NT, MS, MT)
+    gap = jnp.zeros((depth, 256 - kept), jnp.bfloat16)
+    plane_pad = jnp.concatenate([plane_table[:, :kept], gap, plane_table[:, kept:], gap], axis=1)
+    plane_back = plane_table.T
+    row_table, across_table = kernel_tables(width_x, gx_size)
+    row_back = row_table.T
+    chunks = ((0, 8), (8, channels - 8))
+    other_core = [(d, d ^ 1) for d in range(4)]
+    other_y = [(d, d ^ 2) for d in range(4)]
+
+    def forward_chain(planes):
+        sent = []
+        for first, count in chunks:
+            near, far = rows_call(planes, first, count, plane_pad, row_table)
+            near = near + lax.ppermute(far, "gy", other_core)
+            sent.append((near, lax.ppermute(near[MS // 4 :], "gy", other_y)))
+        blocks = []
+        for near, other in sent:
+            packed = pack_call(near, other)
+            blocks.append(lax.all_to_all(packed, "gx", split_axis=0, concat_axis=0, tiled=True))
+        return blocks
+
+    def inverse_chain(blocks):
+        pieces = []
+        for block in blocks:
+            moved = lax.all_to_all(block, "gx", split_axis=0, concat_axis=0, tiled=True)
+            own = unpack_call(moved, width_x)
+            beside = lax.ppermute(own, "gy", other_y)
+            pieces.append(
+                [
+                    own,
+                    beside,
+                    lax.ppermute(own, "gy", other_core),
+                    lax.ppermute(beside, "gy", other_core),
+                ]
+            )
+        return pieces
+
+    modes, *mixed = apply_call(forward_chain(field), across_table, spectral_weight)
+    upstream = cells_call(
+        inverse_chain(mixed), row_back, plane_back, local_weight.T, field, cotangent, bias
+    )
+    grad_weight, *back = adjoint_call(
+        forward_chain(upstream), across_table, spectral_weight, modes
+    )
+    result = cells_call(inverse_chain(back), row_back, plane_back, local_weight, upstream)
+    return (result, grad_weight)
+
+
 def solution(mesh):
     in_specs = (
         P(None, "gx", "gy", None),
@@ -156,4 +544,6 @@
         P(),
     )
     out_specs = (P(None, "gx", "gy", None), P(None, None, None, None, ("gy", "gx")))
-    return jax.shard_map(local, mesh=mesh, in_specs=in_specs, out_specs=out_specs, check_vma=False)
+    width_x, four_rows = NX // mesh.shape["gx"], mesh.shape["gy"] == 4
+    body = local_kernels if four_rows and width_x == 16 else local
+    return jax.shard_map(body, mesh=mesh, in_specs=in_specs, out_specs=out_specs, check_vma=False)

time: 1130 us -> 531 us (0.47); the launches traced: 1110 us -> 526 us
  local copies, waits for them, and re-layouts: 382 us -> 22.9 us
  matrix products: 250 us -> 0 us
  Pallas kernels: 0 us -> 239 us
  blocking collectives: 207 us -> 77.6 us
  other arithmetic: 108 us -> 15.5 us
  starting transfers between devices: 0.16 us -> 40.9 us
  waiting for transfers between devices: 151 us -> 129 us
  between operations: 14.6 us -> 1.02 us
    dot_general x22 -> x0, matrix products: 250 us -> none  [the longest x2 82.7 us: inverse_chain(): lax.dot_general(flattened, plane_table, (((1,), (1,)), ((), ())), preferr...]
    pallas_call x0 -> x16, Pallas kernels: none -> 239 us  [the longest x2 107 us: cells_call(): pl.pallas_call(functools.partial(cells_kernel, counts, bias is not None),...]
    reshape x12 -> x0, local copies, waits for them, and re-layouts: 136 us -> none  [the longest x4 89.2 us: forward_chain(): coeffs.astype(jnp.bfloat16)]
    reduce_scatter x2 -> x0, waiting for transfers between devices: 130 us -> none  [forward_chain(): lax.psum_scatter(partial_terms.astype(jnp.bfloat16), 'gy', scatter_dimens...]
    all_to_all x4 -> x3, blocking collectives: 207 us -> 77.6 us  [the longest x2 50.8 us: inverse_chain(): moved = lax.all_to_all(block, 'gx', split_axis=0, concat_axis=0, tiled=True)]
    ppermute x0 -> x20, waiting for transfers between devices: none -> 97.7 us  [the longest x4 66 us: forward_chain(): sent.append((near, lax.ppermute(near[MS // 4:], 'gy', other_y)))]
    another operation x18 -> x0, other arithmetic: 84.2 us -> none
    unnamed x28 -> x46, local copies, waits for them, and re-layouts: 89.6 us -> 7.89 us
  transfers between devices with their start and end apart: 4 -> 25, of which waited for: 4 -> 12; matrix products, arithmetic and copies ran while one was open for 7% -> 4% of each run, Pallas kernels for 0% -> 14%
where the time goes in v1:
time: 531 us; the launch traced here: 526 us
  Pallas kernels  239 us (45%)
  waiting for transfers between devices  129 us (24%)
  blocking collectives  77.6 us (15%)
  starting transfers between devices  40.9 us (8%)
  local copies, waits for them, and re-layouts  22.9 us (4%)
  other arithmetic  15.5 us (3%)
    pallas_call x2, Pallas kernels, cells_call(): pl.pallas_call(functools.partial(cells_kernel, counts, bias is not None),...  107 us
    ppermute x4, waiting for transfers between devices, forward_chain(): sent.append((near, lax.ppermute(near[MS // 4:], 'gy', other_y)))  66 us
    pallas_call x4, Pallas kernels, rows_call(): pl.pallas_call(rows_kernel, grid=(count // step,), in_specs=[pl.BlockSpec...  56.6 us
    all_to_all x2, blocking collectives, inverse_chain(): moved = lax.all_to_all(block, 'gx', split_axis=0, concat_axis=0, tiled=True)  50.8 us
    ppermute x4, waiting for transfers between devices, inverse_chain(): beside = lax.ppermute(own, 'gy', other_y)  31.1 us
    all_to_all x1, blocking collectives, forward_chain(): lax.all_to_all(packed, 'gx', split_axis=0, concat_axis=0, tiled=True)  26.8 us
    pallas_call x1, Pallas kernels, adjoint_call(): pl.pallas_call(functools.partial(adjoint_kernel, len(blocks)), grid=(chan...  20.8 us
    pallas_call x4, Pallas kernels, pack_call(): pl.pallas_call(pack_kernel, grid=(share,), in_specs=[block, block], out_s...  19.7 us
  transfers between devices with their start and end apart: 25, of which 12 were waited for; matrix products, arithmetic and copies ran while one was open for 4% of the time, Pallas kernels for 14%

profile of v1, /device:TPU:0, one launch (start us, length us, event | category | flops | bytes accessed | tf_op | source)
XLA Modules:
  0.0 526.0 jit_solution(15572779728421202005)
XLA Ops:
  10.4 11.9 %shard_map.77 = (bf16[12,8,16,384]{3,2,1,0:T(8,128)(2,1)}, bf16[12,8,16,384]{3,2,1,0:T(8,128)(2,1)}) custom-call(bf16[20,16,32,1024]{3,2,1,0:T(8,128)(2,1)} %refs_11_.1, bf16[1024,512]{1,0:T(8,128)(2,1)} %copy.35.plane_ref, bf16[384,256]{1,0:T(8,128)(2,1)} %copy.36.row_ref), custom_call_target="tpu_custom_call" | custom-call | flops 6442450944 | bytes 8388608 | tf_op jit(solution)/shard_map/pallas_call | solution.py:218
  22.8 16.4 %shard_map.79 = (bf16[12,12,16,384]{3,2,1,0:T(8,128)(2,1)}, bf16[12,12,16,384]{3,2,1,0:T(8,128)(2,1)}) custom-call(bf16[20,16,32,1024]{3,2,1,0:T(8,128)(2,1)} %refs_11_.1, bf16[1024,512]{1,0:T(8,128)(2,1)} %copy.35.plane_ref, bf16[384,256]{1,0:T(8,128)(2,1)} %copy.36.row_ref), custom_call_target="tpu_custom_call" | custom-call | flops 9663676416 | bytes 12582912 | tf_op jit(solution)/shard_map/pallas_call | solution.py:218
  42.7 13.6 %collective-permute-done.1.other_ref = bf16[6,8,16,384]{3,2,1,0:T(8,128)(2,1)S(1)} collective-permute-done((bf16[6,8,16,384]{3,2,1,0:T(8,128)(2,1)S(1)}, bf16[6,8,16,384]{3,2,1,0:T(8,128)(2,1)S(1)}, u32[]{:S(2)}, u32[]{:S(2)}) %collective-permute-start.1) | collective-permute-done | bytes 589856 | tf_op jit(solution)/shard_map/ppermute | solution.py:504
  57.1 4.8 shard_map.78
  61.9 6.0 %all-to-all-start = ((bf16[8,144,256]{2,1,0:T(8,128)(2,1)}), bf16[8,144,256]{2,1,0:T(8,128)(2,1)S(1)}, u32[]{:S(2)}, u32[]{:S(2)}) async-start(bf16[8,144,256]{2,1,0:T(8,128)(2,1)} %bitcast.39), calls=%async_computation | async-start | bytes 1179648 | tf_op jit(solution)/shard_map/all_to_all | solution.py:508
  71.6 19.0 %collective-permute-done.3.other_ref = bf16[6,12,16,384]{3,2,1,0:T(8,128)(2,1)S(1)} collective-permute-done((bf16[6,12,16,384]{3,2,1,0:T(8,128)(2,1)S(1)}, bf16[6,12,16,384]{3,2,1,0:T(8,128)(2,1)S(1)}, u32[]{:S(2)}, u32[]{:S(2)}) %collective-permute-start.3) | collective-permute-done | bytes 884768 | tf_op jit(solution)/shard_map/ppermute | solution.py:504
  91.5 5.1 shard_map.80
  97.5 5.7 %all-to-all-start.1 = ((bf16[8,144,384]{2,1,0:T(8,128)(2,1)}), bf16[8,144,384]{2,1,0:T(8,128)(2,1)S(1)}, u32[]{:S(2)}, u32[]{:S(2)}) async-start(bf16[8,144,384]{2,1,0:T(8,128)(2,1)} %bitcast.31), calls=%async_computation.1 | async-start | bytes 1769472 | tf_op jit(solution)/shard_map/all_to_all | solution.py:508
  109.0 14.6 %all-to-all-done.1 = bf16[8,144,384]{2,1,0:T(8,128)(2,1)S(1)} async-done(((bf16[8,144,384]{2,1,0:T(8,128)(2,1)}), bf16[8,144,384]{2,1,0:T(8,128)(2,1)S(1)}, u32[]{:S(2)}, u32[]{:S(2)}) %all-to-all-start.1) | async-done | bytes 884768 | tf_op jit(solution)/shard_map/all_to_all | solution.py:508
  124.5 16.6 %shard_map.81 = (f32[2,20,24,144]{3,2,1,0:T(8,128)}, bf16[1152,256]{1,0:T(8,128)(2,1)}, bf16[1152,384]{1,0:T(8,128)(2,1)}) custom-call(bf16[1152,256]{1,0:T(8,128)(2,1)} %bitcast.35, bf16[1152,384]{1,0:T(8,128)(2,1)} %bitcast.29, bf16[192,1024]{1,0:T(8,128)(2,1)} %copy.40.refs_2_, bf16[2,20,20,24,144]{4,3,2,1,0:T(8,128)(2,1)} %refs_3_.3), custom_call_target="tpu_custom_call" | custom-call | tf_op jit(solution)/shard_map/pallas_call | solution.py:352
  141.1 25.6 %all_to_all.88 = bf16[8,144,384]{2,1,0:T(8,128)(2,1)} all-to-all(bf16[8,144,384]{2,1,0:T(8,128)(2,1)} %bitcast.42), channel_id=1, replica_groups=mesh['gx'=8,'gy'=4] {'gx'}, dimensions={0} | all-to-all | bytes 1769472 | tf_op jit(solution)/shard_map/all_to_all | solution.py:514
  170.4 4.8 shard_map.83.refs_4_
  176.7 8.3 %all-to-all-done.2 = bf16[8,144,256]{2,1,0:T(8,128)(2,1)S(1)} async-done(((bf16[8,144,256]{2,1,0:T(8,128)(2,1)}), bf16[8,144,256]{2,1,0:T(8,128)(2,1)S(1)}, u32[]{:S(2)}, u32[]{:S(2)}) %all-to-all-start.2) | async-done | bytes 589856 | tf_op jit(solution)/shard_map/all_to_all | solution.py:514
  185.8 4.5 shard_map.82.refs_0_
  191.9 6.2 %collective-permute-done.7.refs_5_ = bf16[6,12,16,384]{3,2,1,0:T(8,128)(2,1)} collective-permute-done((bf16[6,12,16,384]{3,2,1,0:T(8,128)(2,1)}, bf16[6,12,16,384]{3,2,1,0:T(8,128)(2,1)}, u32[]{:S(2)}, u32[]{:S(2)}) %collective-permute-start.7) | collective-permute-done | bytes 884768 | tf_op jit(solution)/shard_map/ppermute | solution.py:516
  198.6 9.4 %collective-permute-done.4.refs_1_ = bf16[6,8,16,384]{3,2,1,0:T(8,128)(2,1)} collective-permute-done((bf16[6,8,16,384]{3,2,1,0:T(8,128)(2,1)}, bf16[6,8,16,384]{3,2,1,0:T(8,128)(2,1)}, u32[]{:S(2)}, u32[]{:S(2)}) %collective-permute-start.4) | collective-permute-done | bytes 589856 | tf_op jit(solution)/shard_map/ppermute | solution.py:516
  215.9 58.4 %shard_map.84.planes_ref.refs_11_ = bf16[20,16,32,1024]{3,2,1,0:T(8,128)(2,1)} custom-call(bf16[6,8,16,384]{3,2,1,0:T(8,128)(2,1)} %shard_map.82.refs_0_, bf16[6,8,16,384]{3,2,1,0:T(8,128)(2,1)} %collective-permute-done.4.refs_1_, bf16[6,8,16,384]{3,2,1,0:T(8,128)(2,1)} %collective-permute-done.5.refs_2_, ...), custom_call_target="tpu_custom_call" | custom-call | tf_op jit(solution)/shard_map/pallas_call | solution.py:470
  274.3 11.9 %shard_map.85 = (bf16[12,8,16,384]{3,2,1,0:T(8,128)(2,1)}, bf16[12,8,16,384]{3,2,1,0:T(8,128)(2,1)}) custom-call(bf16[20,16,32,1024]{3,2,1,0:T(8,128)(2,1)} %shard_map.84.planes_ref.refs_11_, bf16[1024,512]{1,0:T(8,128)(2,1)} %copy.35.plane_ref, bf16[384,256]{1,0:T(8,128)(2,1)} %copy.36.row_ref), custom_call_target="tpu_custom_call" | custom-call | flops 6442450944 | bytes 8388608 | tf_op jit(solution)/shard_map/pallas_call | solution.py:218
  286.7 16.4 %shard_map.87 = (bf16[12,12,16,384]{3,2,1,0:T(8,128)(2,1)}, bf16[12,12,16,384]{3,2,1,0:T(8,128)(2,1)}) custom-call(bf16[20,16,32,1024]{3,2,1,0:T(8,128)(2,1)} %shard_map.84.planes_ref.refs_11_, bf16[1024,512]{1,0:T(8,128)(2,1)} %copy.35.plane_ref, bf16[384,256]{1,0:T(8,128)(2,1)} %copy.36.row_ref), custom_call_target="tpu_custom_call" | custom-call | flops 9663676416 | bytes 12582912 | tf_op jit(solution)/shard_map/pallas_call | solution.py:218
  305.2 14.1 %collective-permute-done.11.other_ref = bf16[6,8,16,384]{3,2,1,0:T(8,128)(2,1)S(1)} collective-permute-done((bf16[6,8,16,384]{3,2,1,0:T(8,128)(2,1)S(1)}, bf16[6,8,16,384]{3,2,1,0:T(8,128)(2,1)S(1)}, u32[]{:S(2)}, u32[]{:S(2)}) %collective-permute-start.11) | collective-permute-done | bytes 589856 | tf_op jit(solution)/shard_map/ppermute | solution.py:504
  320.1 4.8 shard_map.86
  324.9 5.7 %all-to-all-start.4 = ((bf16[8,144,256]{2,1,0:T(8,128)(2,1)}), bf16[8,144,256]{2,1,0:T(8,128)(2,1)S(1)}, u32[]{:S(2)}, u32[]{:S(2)}) async-start(bf16[8,144,256]{2,1,0:T(8,128)(2,1)} %bitcast.40), calls=%async_computation.4 | async-start | bytes 1179648 | tf_op jit(solution)/shard_map/all_to_all | solution.py:508
  334.8 19.3 %collective-permute-done.13.other_ref = bf16[6,12,16,384]{3,2,1,0:T(8,128)(2,1)S(1)} collective-permute-done((bf16[6,12,16,384]{3,2,1,0:T(8,128)(2,1)S(1)}, bf16[6,12,16,384]{3,2,1,0:T(8,128)(2,1)S(1)}, u32[]{:S(2)}, u32[]{:S(2)}) %collective-permute-start.13) | collective-permute-done | bytes 884768 | tf_op jit(solution)/shard_map/ppermute | solution.py:504
  355.0 5.1 shard_map.88
  360.1 26.8 %all_to_all.89 = bf16[8,144,384]{2,1,0:T(8,128)(2,1)} all-to-all(bf16[8,144,384]{2,1,0:T(8,128)(2,1)} %bitcast.32), channel_id=1, replica_groups=mesh['gx'=8,'gy'=4] {'gx'}, dimensions={0} | all-to-all | bytes 1769472 | tf_op jit(solution)/shard_map/all_to_all | solution.py:508
  386.9 20.8 %shard_map.89 = (f32[2,20,20,24,144]{4,3,2,1,0:T(8,128)}, bf16[1152,256]{1,0:T(8,128)(2,1)}, bf16[1152,384]{1,0:T(8,128)(2,1)}) custom-call(bf16[1152,256]{1,0:T(8,128)(2,1)} %bitcast.36, bf16[1152,384]{1,0:T(8,128)(2,1)} %bitcast.30, bf16[192,1024]{1,0:T(8,128)(2,1)} %copy.40.refs_2_, bf16[2,20,20,24,144]{4,3,2,1,0:T(8,128)(2,1)} %refs_3_.3, ...), custom_call_target="tpu_custom_call" | custom-call | tf_op jit(solution)/shard_map/pallas_call | solution.py:401
  407.7 25.2 %all_to_all.90 = bf16[8,144,384]{2,1,0:T(8,128)(2,1)} all-to-all(bf16[8,144,384]{2,1,0:T(8,128)(2,1)} %bitcast.41), channel_id=1, replica_groups=mesh['gx'=8,'gy'=4] {'gx'}, dimensions={0} | all-to-all | bytes 1769472 | tf_op jit(solution)/shard_map/all_to_all | solution.py:514
  436.6 4.8 shard_map.91.refs_4_
  442.9 8.1 %all-to-all-done.6 = bf16[8,144,256]{2,1,0:T(8,128)(2,1)S(1)} async-done(((bf16[8,144,256]{2,1,0:T(8,128)(2,1)}), bf16[8,144,256]{2,1,0:T(8,128)(2,1)S(1)}, u32[]{:S(2)}, u32[]{:S(2)}) %all-to-all-start.6) | async-done | bytes 589856 | tf_op jit(solution)/shard_map/all_to_all | solution.py:514
  457.9 6.4 %collective-permute-done.17.refs_5_ = bf16[6,12,16,384]{3,2,1,0:T(8,128)(2,1)} collective-permute-done((bf16[6,12,16,384]{3,2,1,0:T(8,128)(2,1)}, bf16[6,12,16,384]{3,2,1,0:T(8,128)(2,1)}, u32[]{:S(2)}, u32[]{:S(2)}) %collective-permute-start.17) | collective-permute-done | bytes 884768 | tf_op jit(solution)/shard_map/ppermute | solution.py:516
  464.8 9.1 %collective-permute-done.14.refs_1_ = bf16[6,8,16,384]{3,2,1,0:T(8,128)(2,1)} collective-permute-done((bf16[6,8,16,384]{3,2,1,0:T(8,128)(2,1)}, bf16[6,8,16,384]{3,2,1,0:T(8,128)(2,1)}, u32[]{:S(2)}, u32[]{:S(2)}) %collective-permute-start.14) | collective-permute-done | bytes 589856 | tf_op jit(solution)/shard_map/ppermute | solution.py:516
  477.3 48.7 %shard_map.92 = bf16[20,16,32,1024]{3,2,1,0:T(8,128)(2,1)} custom-call(bf16[6,8,16,384]{3,2,1,0:T(8,128)(2,1)} %shard_map.90.refs_0_, bf16[6,8,16,384]{3,2,1,0:T(8,128)(2,1)} %collective-permute-done.14.refs_1_, bf16[6,8,16,384]{3,2,1,0:T(8,128)(2,1)} %collective-permute-done.15.refs_2_, bf16[6,8,16,384]{3,2,1,0:T(8,128)(2,1)} %collective-permute-done.16.refs_3_, ...), custom_call_target="tpu_custom_call" | custom-call | tf_op jit(solution)/shard_map/pallas_call | solution.py:470
  (135 shorter events, 66.9 us)
Async XLA Ops:
  22.3 17.0 %copy-start.13 = (bf16[12,8,16,384]{3,2,1,0:T(8,128)(2,1)S(1)}, bf16[12,8,16,384]{3,2,1,0:T(8,128)(2,1)}, u32[]{:S(2)}) copy-start(bf16[12,8,16,384]{3,2,1,0:T(8,128)(2,1)} %get-tuple-element.17) | copy-start | bytes 3538948
  22.3 17.0 %collective-permute-start = (bf16[12,8,16,384]{3,2,1,0:T(8,128)(2,1)}, bf16[12,8,16,384]{3,2,1,0:T(8,128)(2,1)S(1)}, u32[]{:S(2)}, u32[]{:S(2)}) collective-permute-start(bf16[12,8,16,384]{3,2,1,0:T(8,128)(2,1)} %get-tuple-element.18), channel_id=1, source_target_pairs={{0,1},{1,0},{2,3},{3,2},{4,5},{5,4},{6,7},{7,6},{8,9},{9,8},{10,11... | collective-permute-start | bytes 3538952 | tf_op jit(solution)/shard_map/ppermute | solution.py:503
  39.2 28.7 %collective-permute-start.2 = (bf16[12,12,16,384]{3,2,1,0:T(8,128)(2,1)}, bf16[12,12,16,384]{3,2,1,0:T(8,128)(2,1)}, u32[]{:S(2)}, u32[]{:S(2)}) collective-permute-start(bf16[12,12,16,384]{3,2,1,0:T(8,128)(2,1)} %get-tuple-element.20), channel_id=1, source_target_pairs={{0,1},{1,0},{2,3},{3,2},{4,5},{5,4},{6,7},{7,6},{8,9},{9,8},{10,11... | collective-permute-start | bytes 5308424 | tf_op jit(solution)/shard_map/ppermute | solution.py:503
  39.7 28.2 %copy-start.11 = (bf16[12,12,16,384]{3,2,1,0:T(8,128)(2,1)S(1)}, bf16[12,12,16,384]{3,2,1,0:T(8,128)(2,1)}, u32[]{:S(2)}) copy-start(bf16[12,12,16,384]{3,2,1,0:T(8,128)(2,1)} %get-tuple-element.19) | copy-start | bytes 5308420
  39.7 16.6 %collective-permute-start.1 = (bf16[6,8,16,384]{3,2,1,0:T(8,128)(2,1)S(1)}, bf16[6,8,16,384]{3,2,1,0:T(8,128)(2,1)S(1)}, u32[]{:S(2)}, u32[]{:S(2)}) collective-permute-start(bf16[6,8,16,384]{3,2,1,0:T(8,128)(2,1)S(1)} %slice.32), channel_id=1, source_target_pairs={{0,2},{1,3},{2,0},{3,1},{4,6},{5,7},{6,4},{7,5},{8,10},{9,11},{10,... | collective-permute-start | bytes 1769480 | tf_op jit(solution)/shard_map/ppermute | solution.py:504
  61.9 34.7 %all-to-all-start = ((bf16[8,144,256]{2,1,0:T(8,128)(2,1)}), bf16[8,144,256]{2,1,0:T(8,128)(2,1)S(1)}, u32[]{:S(2)}, u32[]{:S(2)}) async-start(bf16[8,144,256]{2,1,0:T(8,128)(2,1)} %bitcast.39), calls=%async_computation | async-start | bytes 1179648 | tf_op jit(solution)/shard_map/all_to_all | solution.py:508
  69.9 20.7 %copy-start = (bf16[12,12,16,384]{3,2,1,0:T(8,128)(2,1)}, bf16[12,12,16,384]{3,2,1,0:T(8,128)(2,1)S(1)}, u32[]{:S(2)}) copy-start(bf16[12,12,16,384]{3,2,1,0:T(8,128)(2,1)S(1)} %add.190.own_ref) | copy-start | bytes 5308420
  70.0 20.6 %collective-permute-start.3 = (bf16[6,12,16,384]{3,2,1,0:T(8,128)(2,1)S(1)}, bf16[6,12,16,384]{3,2,1,0:T(8,128)(2,1)S(1)}, u32[]{:S(2)}, u32[]{:S(2)}) collective-permute-start(bf16[6,12,16,384]{3,2,1,0:T(8,128)(2,1)S(1)} %slice.33), channel_id=1, source_target_pairs={{0,2},{1,3},{2,0},{3,1},{4,6},{5,7},{6,4},{7,5},{8,10},{9,11},{10,... | collective-permute-start | bytes 2654216 | tf_op jit(solution)/shard_map/ppermute | solution.py:504
  97.5 26.2 %all-to-all-start.1 = ((bf16[8,144,384]{2,1,0:T(8,128)(2,1)}), bf16[8,144,384]{2,1,0:T(8,128)(2,1)S(1)}, u32[]{:S(2)}, u32[]{:S(2)}) async-start(bf16[8,144,384]{2,1,0:T(8,128)(2,1)} %bitcast.31), calls=%async_computation.1 | async-start | bytes 1769472 | tf_op jit(solution)/shard_map/all_to_all | solution.py:508
  166.7 41.3 %copy-start.21 = (bf16[20,20]{1,0:T(8,128)(2,1)S(1)}, bf16[20,20]{1,0:T(8,128)(2,1)}, u32[]{:S(2)}) copy-start(bf16[20,20]{1,0:T(8,128)(2,1)} %param.11) | copy-start | bytes 2404
  166.7 41.4 %copy-start.22 = (f32[20]{0:T(128)S(1)}, f32[20]{0:T(128)}, u32[]{:S(2)}) copy-start(f32[20]{0:T(128)} %param.12) | copy-start | bytes 244
  166.7 18.3 %all-to-all-start.2 = ((bf16[8,144,256]{2,1,0:T(8,128)(2,1)}), bf16[8,144,256]{2,1,0:T(8,128)(2,1)S(1)}, u32[]{:S(2)}, u32[]{:S(2)}) async-start(bf16[8,144,256]{2,1,0:T(8,128)(2,1)} %bitcast.44), calls=%async_computation.2 | async-start | bytes 1179648 | tf_op jit(solution)/shard_map/all_to_all | solution.py:514
  175.2 22.9 %collective-permute-start.7 = (bf16[6,12,16,384]{3,2,1,0:T(8,128)(2,1)}, bf16[6,12,16,384]{3,2,1,0:T(8,128)(2,1)}, u32[]{:S(2)}, u32[]{:S(2)}) collective-permute-start(bf16[6,12,16,384]{3,2,1,0:T(8,128)(2,1)} %shard_map.83.refs_4_), channel_id=1, source_target_pairs={{0,2},{1,3},{2,0},{3,1},{4,6},{5,7},{6,4},{7,5},{8,10},{9,11},{10,... | collective-permute-start | bytes 2654216 | tf_op jit(solution)/shard_map/ppermute | solution.py:516
  190.4 17.6 %collective-permute-start.4 = (bf16[6,8,16,384]{3,2,1,0:T(8,128)(2,1)}, bf16[6,8,16,384]{3,2,1,0:T(8,128)(2,1)}, u32[]{:S(2)}, u32[]{:S(2)}) collective-permute-start(bf16[6,8,16,384]{3,2,1,0:T(8,128)(2,1)} %shard_map.82.refs_0_), channel_id=1, source_target_pairs={{0,2},{1,3},{2,0},{3,1},{4,6},{5,7},{6,4},{7,5},{8,10},{9,11},{10,... | collective-permute-start | bytes 1769480 | tf_op jit(solution)/shard_map/ppermute | solution.py:516
  191.9 24.0 %collective-permute-start.8 = (bf16[6,12,16,384]{3,2,1,0:T(8,128)(2,1)}, bf16[6,12,16,384]{3,2,1,0:T(8,128)(2,1)}, u32[]{:S(2)}, u32[]{:S(2)}) collective-permute-start(bf16[6,12,16,384]{3,2,1,0:T(8,128)(2,1)} %shard_map.83.refs_4_), channel_id=1, source_target_pairs={{0,1},{1,0},{2,3},{3,2},{4,5},{5,4},{6,7},{7,6},{8,9},{9,8},{10,11... | collective-permute-start | bytes 2654216 | tf_op jit(solution)/shard_map/ppermute | solution.py:521
  198.1 17.8 %collective-permute-start.9 = (bf16[6,12,16,384]{3,2,1,0:T(8,128)(2,1)}, bf16[6,12,16,384]{3,2,1,0:T(8,128)(2,1)}, u32[]{:S(2)}, u32[]{:S(2)}) collective-permute-start(bf16[6,12,16,384]{3,2,1,0:T(8,128)(2,1)} %collective-permute-done.7.refs_5_), channel_id=1, source_target_pairs={{0,1},{1,0},{2,3},{3,2},{4,5},{5,4},{6,7},{7,6},{8,9},{9,8},{10,11... | collective-permute-start | bytes 2654216 | tf_op jit(solution)/shard_map/ppermute | solution.py:522
  198.1 17.7 %collective-permute-start.5 = (bf16[6,8,16,384]{3,2,1,0:T(8,128)(2,1)}, bf16[6,8,16,384]{3,2,1,0:T(8,128)(2,1)}, u32[]{:S(2)}, u32[]{:S(2)}) collective-permute-start(bf16[6,8,16,384]{3,2,1,0:T(8,128)(2,1)} %shard_map.82.refs_0_), channel_id=1, source_target_pairs={{0,1},{1,0},{2,3},{3,2},{4,5},{5,4},{6,7},{7,6},{8,9},{9,8},{10,11... | collective-permute-start | bytes 1769480 | tf_op jit(solution)/shard_map/ppermute | solution.py:521
  208.0 7.9 %collective-permute-start.6 = (bf16[6,8,16,384]{3,2,1,0:T(8,128)(2,1)}, bf16[6,8,16,384]{3,2,1,0:T(8,128)(2,1)}, u32[]{:S(2)}, u32[]{:S(2)}) collective-permute-start(bf16[6,8,16,384]{3,2,1,0:T(8,128)(2,1)} %collective-permute-done.4.refs_1_), channel_id=1, source_target_pairs={{0,1},{1,0},{2,3},{3,2},{4,5},{5,4},{6,7},{7,6},{8,9},{9,8},{10,11... | collective-permute-start | bytes 1769480 | tf_op jit(solution)/shard_map/ppermute | solution.py:522
  286.2 17.0 %collective-permute-start.10 = (bf16[12,8,16,384]{3,2,1,0:T(8,128)(2,1)}, bf16[12,8,16,384]{3,2,1,0:T(8,128)(2,1)S(1)}, u32[]{:S(2)}, u32[]{:S(2)}) collective-permute-start(bf16[12,8,16,384]{3,2,1,0:T(8,128)(2,1)} %get-tuple-element.24), channel_id=1, source_target_pairs={{0,1},{1,0},{2,3},{3,2},{4,5},{5,4},{6,7},{7,6},{8,9},{9,8},{10,11... | collective-permute-start | bytes 3538952 | tf_op jit(solution)/shard_map/ppermute | solution.py:503
  303.1 27.5 %collective-permute-start.12 = (bf16[12,12,16,384]{3,2,1,0:T(8,128)(2,1)}, bf16[12,12,16,384]{3,2,1,0:T(8,128)(2,1)}, u32[]{:S(2)}, u32[]{:S(2)}) collective-permute-start(bf16[12,12,16,384]{3,2,1,0:T(8,128)(2,1)} %get-tuple-element.26), channel_id=1, source_target_pairs={{0,1},{1,0},{2,3},{3,2},{4,5},{5,4},{6,7},{7,6},{8,9},{9,8},{10,11... | collective-permute-start | bytes 5308424 | tf_op jit(solution)/shard_map/ppermute | solution.py:503
  303.6 15.7 %collective-permute-start.11 = (bf16[6,8,16,384]{3,2,1,0:T(8,128)(2,1)S(1)}, bf16[6,8,16,384]{3,2,1,0:T(8,128)(2,1)S(1)}, u32[]{:S(2)}, u32[]{:S(2)}) collective-permute-start(bf16[6,8,16,384]{3,2,1,0:T(8,128)(2,1)S(1)} %slice.34), channel_id=1, source_target_pairs={{0,2},{1,3},{2,0},{3,1},{4,6},{5,7},{6,4},{7,5},{8,10},{9,11},{10,... | collective-permute-start | bytes 1769480 | tf_op jit(solution)/shard_map/ppermute | solution.py:504
  324.9 35.2 %all-to-all-start.4 = ((bf16[8,144,256]{2,1,0:T(8,128)(2,1)}), bf16[8,144,256]{2,1,0:T(8,128)(2,1)S(1)}, u32[]{:S(2)}, u32[]{:S(2)}) async-start(bf16[8,144,256]{2,1,0:T(8,128)(2,1)} %bitcast.40), calls=%async_computation.4 | async-start | bytes 1179648 | tf_op jit(solution)/shard_map/all_to_all | solution.py:508
  333.1 21.0 %copy-start.1 = (bf16[12,12,16,384]{3,2,1,0:T(8,128)(2,1)}, bf16[12,12,16,384]{3,2,1,0:T(8,128)(2,1)S(1)}, u32[]{:S(2)}) copy-start(bf16[12,12,16,384]{3,2,1,0:T(8,128)(2,1)S(1)} %add.193.own_ref) | copy-start | bytes 5308420
  333.2 20.9 %collective-permute-start.13 = (bf16[6,12,16,384]{3,2,1,0:T(8,128)(2,1)S(1)}, bf16[6,12,16,384]{3,2,1,0:T(8,128)(2,1)S(1)}, u32[]{:S(2)}, u32[]{:S(2)}) collective-permute-start(bf16[6,12,16,384]{3,2,1,0:T(8,128)(2,1)S(1)} %slice.35), channel_id=1, source_target_pairs={{0,2},{1,3},{2,0},{3,1},{4,6},{5,7},{6,4},{7,5},{8,10},{9,11},{10,... | collective-permute-start | bytes 2654216 | tf_op jit(solution)/shard_map/ppermute | solution.py:504
  360.1 26.8 %copy-start.8 = (bf16[8,144,256]{2,1,0:T(8,128)(2,1)}, bf16[8,144,256]{2,1,0:T(8,128)(2,1)S(1)}, u32[]{:S(2)}) copy-start(bf16[8,144,256]{2,1,0:T(8,128)(2,1)S(1)} %all-to-all-done.4) | copy-start | bytes 1769476
  432.9 18.1 %all-to-all-start.6 = ((bf16[8,144,256]{2,1,0:T(8,128)(2,1)}), bf16[8,144,256]{2,1,0:T(8,128)(2,1)S(1)}, u32[]{:S(2)}, u32[]{:S(2)}) async-start(bf16[8,144,256]{2,1,0:T(8,128)(2,1)} %bitcast.43), calls=%async_computation.6 | async-start | bytes 1179648 | tf_op jit(solution)/shard_map/all_to_all | solution.py:514
  441.4 22.9 %collective-permute-start.17 = (bf16[6,12,16,384]{3,2,1,0:T(8,128)(2,1)}, bf16[6,12,16,384]{3,2,1,0:T(8,128)(2,1)}, u32[]{:S(2)}, u32[]{:S(2)}) collective-permute-start(bf16[6,12,16,384]{3,2,1,0:T(8,128)(2,1)} %shard_map.91.refs_4_), channel_id=1, source_target_pairs={{0,2},{1,3},{2,0},{3,1},{4,6},{5,7},{6,4},{7,5},{8,10},{9,11},{10,... | collective-permute-start | bytes 2654216 | tf_op jit(solution)/shard_map/ppermute | solution.py:516
  456.4 17.6 %collective-permute-start.14 = (bf16[6,8,16,384]{3,2,1,0:T(8,128)(2,1)}, bf16[6,8,16,384]{3,2,1,0:T(8,128)(2,1)}, u32[]{:S(2)}, u32[]{:S(2)}) collective-permute-start(bf16[6,8,16,384]{3,2,1,0:T(8,128)(2,1)} %shard_map.90.refs_0_), channel_id=1, source_target_pairs={{0,2},{1,3},{2,0},{3,1},{4,6},{5,7},{6,4},{7,5},{8,10},{9,11},{10,... | collective-permute-start | bytes 1769480 | tf_op jit(solution)/shard_map/ppermute | solution.py:516
  457.9 18.4 %collective-permute-start.18 = (bf16[6,12,16,384]{3,2,1,0:T(8,128)(2,1)}, bf16[6,12,16,384]{3,2,1,0:T(8,128)(2,1)S(1)}, u32[]{:S(2)}, u32[]{:S(2)}) collective-permute-start(bf16[6,12,16,384]{3,2,1,0:T(8,128)(2,1)} %shard_map.91.refs_4_), channel_id=1, source_target_pairs={{0,1},{1,0},{2,3},{3,2},{4,5},{5,4},{6,7},{7,6},{8,9},{9,8},{10,11... | collective-permute-start | bytes 2654216 | tf_op jit(solution)/shard_map/ppermute | solution.py:521
  464.3 12.0 %collective-permute-start.19 = (bf16[6,12,16,384]{3,2,1,0:T(8,128)(2,1)}, bf16[6,12,16,384]{3,2,1,0:T(8,128)(2,1)}, u32[]{:S(2)}, u32[]{:S(2)}) collective-permute-start(bf16[6,12,16,384]{3,2,1,0:T(8,128)(2,1)} %collective-permute-done.17.refs_5_), channel_id=1, source_target_pairs={{0,1},{1,0},{2,3},{3,2},{4,5},{5,4},{6,7},{7,6},{8,9},{9,8},{10,11... | collective-permute-start | bytes 2654216 | tf_op jit(solution)/shard_map/ppermute | solution.py:522
  464.3 11.4 %collective-permute-start.15 = (bf16[6,8,16,384]{3,2,1,0:T(8,128)(2,1)}, bf16[6,8,16,384]{3,2,1,0:T(8,128)(2,1)}, u32[]{:S(2)}, u32[]{:S(2)}) collective-permute-start(bf16[6,8,16,384]{3,2,1,0:T(8,128)(2,1)} %shard_map.90.refs_0_), channel_id=1, source_target_pairs={{0,1},{1,0},{2,3},{3,2},{4,5},{5,4},{6,7},{7,6},{8,9},{9,8},{10,11... | collective-permute-start | bytes 1769480 | tf_op jit(solution)/shard_map/ppermute | solution.py:521
  474.0 2.3 collective-permute-start.16
  (16 other events, 67.5 us)
